TPU v7x, 32 devices: a whole 2x2x4 slice. The times are simulated.
32 devices in a mesh: node: 8 (over z, y), head: 4 (over x, core).
Axes of the slice: x: 2, y: 2, z: 4, core: 2. Of those that a mesh axis runs over, the one named last changes fastest.
Arguments:
- features: bfloat16 [16384, 256], P(('node', 'head')), may hold values from -40 to 40
- in_weight: bfloat16 [256, 768], replicated, may hold values from -0.6 to 0.6
- out_weight: bfloat16 [256, 256], replicated, may hold values from -0.375 to 0.375
- cotangent: bfloat16 [16384, 256], P(('node', 'head')), may hold values from -6 to 6
- key_slots: int32 [128, 12], P('node'), may hold values from 0 to 31, as said below
- block_count: int32 [128], P('node'), may hold values from 1 to 12
- wanted: int32 [8, 8, 2], P('node'), may hold values from 0 to 15
Outputs:
- output: bfloat16 [16384, 256], P(('node', 'head'))
- feature_grad: bfloat16 [16384, 256], P(('node', 'head'))
- in_weight_grad: float32 [256, 768], P(None, 'head')
- out_weight_grad: float32 [256, 256], P('head')
Inputs may be any that keep to these rules, and one draw needn't show every extreme that they name: `key_slots`: slot 0 of a query block names the block itself; the slots of one query block are distinct.
All inputs are finite; a program needn't handle non-finite values.
Results may differ from a plain program's by a relative error of at most 0.02.
The roundings to bfloat16 on the way count: a program that leaves them out, or rounds other values in their place, can miss the bound.
Values may be sent and summed in bfloat16 or wider, within the bound.
No kernel may reach another device: no remote copies, remote signals or barrier semaphores. Data moves between devices by JAX's collectives and lax.ppermute only.
A program may use at most 128 MiB of HBM per device.

v0:
```python
import math

import jax
import jax.numpy as jnp
from jax import lax
from jax.sharding import PartitionSpec as P

HEADS = 4
HD = 64
BLOCK = 128
BLK = 16
PER = 12
CAP = 2


def attention_weights(query_block, key_block, live_mask, score_scale):
    scores = (
        jnp.einsum("gqhd,gpkhd->ghqpk", query_block, key_block, preferred_element_type=jnp.float32)
        * score_scale
    )
    scores = jnp.where(live_mask[:, None, None, :, None], scores, -1e30)
    layout = scores.shape
    scores = scores.reshape(layout[0], layout[1], layout[2], layout[3] * layout[4])
    highest = jnp.max(scores, axis=-1, keepdims=True)
    raised = jnp.exp(scores - highest)
    return (raised / jnp.sum(raised, axis=-1, keepdims=True)).reshape(layout)


def on_device(features, in_weight, out_weight, cotangent, key_slots, block_count, wanted):
    head_count = lax.axis_size("head")
    node_count = lax.axis_size("node")
    row_count = features.shape[0]
    local_heads = HEADS // head_count
    node_rows = row_count * head_count
    total_nodes = node_rows * node_count
    head_width = local_heads * 3 * HD
    score_scale = HD ** (-0.5)
    projected = jnp.dot(features, in_weight, preferred_element_type=jnp.float32).astype(
        jnp.bfloat16
    )
    projected = lax.all_to_all(projected, "head", split_axis=1, concat_axis=0, tiled=True)
    projected = projected.reshape(BLK, BLOCK, local_heads, 3, HD)
    queries = projected[:, :, :, 0]
    paired = projected[:, :, :, 1:].reshape(BLK, BLOCK, local_heads * 2 * HD)
    requests = lax.all_to_all(wanted, "node", split_axis=1, concat_axis=0, tiled=True).reshape(-1)
    outgoing = paired[requests].reshape(node_count, CAP, BLOCK, local_heads * 2 * HD)
    incoming = lax.all_to_all(outgoing, "node", split_axis=0, concat_axis=0, tiled=True)
    table = jnp.concatenate(
        [paired, incoming.reshape(node_count * CAP, BLOCK, local_heads * 2 * HD)], axis=0
    )
    group_size = math.gcd(BLK, max(1, 512 // BLOCK))
    step_count = BLK // group_size
    live_slots = jnp.arange(PER, dtype=jnp.int32)[None, :] < block_count[:, None]
    query_groups = queries.reshape(step_count, group_size, BLOCK, local_heads, HD)
    slot_groups = key_slots.reshape(step_count, group_size, PER)
    live_groups = live_slots.reshape(step_count, group_size, PER)

    def fetch_keys(slots):
        chosen = table[slots.reshape(-1)].reshape(group_size, PER, BLOCK, local_heads, 2, HD)
        return (chosen[:, :, :, :, 0], chosen[:, :, :, :, 1])

    def forward_step(inputs):
        query_block, slots, live_mask = inputs
        key_block, value_block = fetch_keys(slots)
        attention = attention_weights(query_block, key_block, live_mask, score_scale)
        result = jnp.einsum(
            "ghqpk,gpkhd->gqhd",
            attention.astype(jnp.bfloat16),
            value_block,
            preferred_element_type=jnp.float32,
        )
        return result.astype(jnp.bfloat16)

    attended = lax.map(forward_step, (query_groups, slot_groups, live_groups)).reshape(
        node_rows, local_heads * HD
    )
    attended_rows = lax.all_to_all(attended, "head", split_axis=0, concat_axis=1, tiled=True)
    summed = features.astype(jnp.float32) + jnp.dot(
        attended_rows, out_weight, preferred_element_type=jnp.float32
    )
    root_mean = jnp.sqrt(jnp.mean(summed * summed, axis=-1, keepdims=True) + 1e-06)
    normed = summed / root_mean
    output = normed.astype(jnp.bfloat16)
    upstream = cotangent.astype(jnp.float32)
    norm_grad = (
        upstream - normed * jnp.mean(upstream * normed, axis=-1, keepdims=True)
    ) / root_mean
    norm_grad_low = norm_grad.astype(jnp.bfloat16)
    out_weight_grad = jnp.dot(attended_rows.T, norm_grad_low, preferred_element_type=jnp.float32)
    attended_grad = jnp.dot(norm_grad_low, out_weight.T, preferred_element_type=jnp.float32).astype(
        jnp.bfloat16
    )
    attended_grad = lax.all_to_all(attended_grad, "head", split_axis=1, concat_axis=0, tiled=True)
    grad_blocks = attended_grad.reshape(BLK, BLOCK, local_heads, HD)
    attended_blocks = attended.reshape(BLK, BLOCK, local_heads, HD)
    row_dots = jnp.sum(
        grad_blocks.astype(jnp.float32) * attended_blocks.astype(jnp.float32), axis=-1
    )
    grad_groups = grad_blocks.reshape(step_count, group_size, BLOCK, local_heads, HD)
    dot_groups = row_dots.reshape(step_count, group_size, BLOCK, local_heads)

    def backward_step(accumulated, inputs):
        query_block, slots, live_mask, grad_block, dot_block = inputs
        key_block, value_block = fetch_keys(slots)
        attention = attention_weights(query_block, key_block, live_mask, score_scale)
        attention_low = attention.astype(jnp.bfloat16)
        prob_grad = jnp.einsum(
            "gqhd,gpkhd->ghqpk", grad_block, value_block, preferred_element_type=jnp.float32
        )
        row_term = jnp.transpose(dot_block, (0, 2, 1))[:, :, :, None, None]
        score_grad = (attention * (prob_grad - row_term) * score_scale).astype(jnp.bfloat16)
        query_grad = jnp.einsum(
            "ghqpk,gpkhd->gqhd", score_grad, key_block, preferred_element_type=jnp.float32
        )
        key_grad = jnp.einsum(
            "ghqpk,gqhd->gpkhd", score_grad, query_block, preferred_element_type=jnp.float32
        )
        value_grad = jnp.einsum(
            "ghqpk,gqhd->gpkhd", attention_low, grad_block, preferred_element_type=jnp.float32
        )
        pair_grads = jnp.stack([key_grad, value_grad], axis=4).reshape(
            group_size * PER, BLOCK, local_heads * 2 * HD
        )
        accumulated = accumulated.at[slots.reshape(-1)].add(pair_grads)
        return (accumulated, query_grad.astype(jnp.bfloat16))

    blank = jnp.zeros((BLK + node_count * CAP, BLOCK, local_heads * 2 * HD), jnp.float32)
    accumulated, query_grads = lax.scan(
        backward_step, blank, (query_groups, slot_groups, live_groups, grad_groups, dot_groups)
    )
    leaving = (
        accumulated[BLK:].astype(jnp.bfloat16).reshape(node_count, CAP, BLOCK, local_heads * 2 * HD)
    )
    returned = lax.all_to_all(leaving, "node", split_axis=0, concat_axis=0, tiled=True)
    returned = returned.astype(jnp.float32).reshape(node_count * CAP, BLOCK, local_heads * 2 * HD)
    pair_grad_sums = accumulated[:BLK].at[requests].add(returned)
    pair_grad_sums = pair_grad_sums.astype(jnp.bfloat16).reshape(BLK, BLOCK, local_heads, 2, HD)
    query_grads = query_grads.reshape(BLK, BLOCK, local_heads, 1, HD)
    projected_grad = jnp.concatenate([query_grads, pair_grad_sums], axis=3).reshape(
        node_rows, head_width
    )
    grad_rows_back = lax.all_to_all(projected_grad, "head", split_axis=0, concat_axis=1, tiled=True)
    feature_grad = norm_grad + jnp.dot(
        grad_rows_back, in_weight.T, preferred_element_type=jnp.float32
    )
    in_weight_grad = jnp.dot(features.T, grad_rows_back, preferred_element_type=jnp.float32)
    in_weight_grad, out_weight_grad = (
        lax.psum_scatter(in_weight_grad, "head", scatter_dimension=1, tiled=True),
        lax.psum_scatter(out_weight_grad, "head", scatter_dimension=0, tiled=True),
    )
    in_weight_grad, out_weight_grad = lax.psum((in_weight_grad, out_weight_grad), "node")
    grad_factor = total_nodes ** (-0.5)
    return (
        output,
        feature_grad.astype(jnp.bfloat16),
        in_weight_grad * grad_factor,
        out_weight_grad * grad_factor,
    )


def solution(mesh):
    placed = (
        P(("node", "head"), None),
        P(),
        P(),
        P(("node", "head"), None),
        P("node", None),
        P("node"),
        P("node", None, None),
    )
    return jax.shard_map(
        on_device,
        mesh=mesh,
        in_specs=placed,
        out_specs=(
            P(("node", "head"), None),
            P(("node", "head"), None),
            P(None, "head"),
            P("head", None),
        ),
        check_vma=False,
    )
```

profile of v0, /device:TPU:0, one launch (start us, length us, event | category | flops | bytes accessed | tf_op | source)
XLA Modules:
  0.0 376.0 jit_solution(13005593242906488008)
XLA Ops:
  8.6 7.3 %all-to-all-start.1 = ((s32[1,8,2]{2,0,1:T(1,128)}), s32[1,8,2]{2,0,1:T(1,128)S(1)}, u32[]{:S(2)}, u32[]{:S(2)}) async-start(s32[1,8,2]{2,0,1:T(1,128)} %copy.101), calls=%async_computation.1 | async-start | bytes 8192 | tf_op jit(solution)/shard_map/all_to_all | solution.py:45
  18.4 3.9 %all-to-all-done.1 = s32[1,8,2]{2,0,1:T(1,128)S(1)} async-done(((s32[1,8,2]{2,0,1:T(1,128)}), s32[1,8,2]{2,0,1:T(1,128)S(1)}, u32[]{:S(2)}, u32[]{:S(2)}) %all-to-all-start.1) | async-done | bytes 96 | tf_op jit(solution)/shard_map/all_to_all | solution.py:45
  22.2 3.5 all-to-all-start
  27.0 10.3 %all-to-all-done = bf16[512,4,192]{0,2,1:T(8,128)(2,1)S(1)} async-done(((bf16[512,4,192]{0,2,1:T(8,128)(2,1)}), bf16[512,4,192]{0,2,1:T(8,128)(2,1)S(1)}, u32[]{:S(2)}, u32[]{:S(2)}) %all-to-all-start) | async-done | bytes 786464 | tf_op jit(solution)/shard_map/all_to_all | solution.py:41
  39.9 3.6 all-to-all-start.2
  44.4 13.6 %all-to-all-done.2 = bf16[8,2,128,128]{2,3,1,0:T(8,128)(2,1)S(1)} async-done(((bf16[8,2,128,128]{2,3,1,0:T(8,128)(2,1)}), bf16[8,2,128,128]{2,3,1,0:T(8,128)(2,1)S(1)}, u32[]{:S(2)}, u32[]{:S(2)}) %all-to-all-start.2) | async-done | bytes 524320 | tf_op jit(solution)/shard_map/all_to_all | solution.py:47
  58.8 32.1 %while.22 = (s32[]{:T(128)}, bf16[4,4,128,1,64]{2,1,4,0,3:T(4,128)(2,1)}, s32[4,4,12]{2,1,0:T(4,128)S(1)}, bf16[32,128,128]{2,1,0:T(8,128)(2,1)S(1)}, pred[4,4,1...) while((s32[]{:T(128)}, bf16[4,4,128,1,64]{2,1,4,0,3:T(4,128)(2,1)}, ...), condition=%wide.region_3.4_spmd, body=%wide.region_0.3_spmd.sunk | while | flops 210796688 | bytes 23872272 | solution.py:74
  92.7 3.4 all-to-all-start.3
  97.4 4.7 %all-to-all-done.3 = bf16[4,512,64]{1,2,0:T(8,128)(2,1)S(1)} async-done(((bf16[4,512,64]{1,2,0:T(8,128)(2,1)}), bf16[4,512,64]{1,2,0:T(8,128)(2,1)S(1)}, u32[]{:S(2)}, u32[]{:S(2)}) %all-to-all-start.3) | async-done | bytes 262176 | tf_op jit(solution)/shard_map/all_to_all | solution.py:77
  106.1 3.6 all-to-all-start.4
  109.7 5.8 %all-to-all-done.4 = bf16[512,4,64]{0,2,1:T(8,128)(2,1)S(1)} async-done(((bf16[512,4,64]{0,2,1:T(8,128)(2,1)}), bf16[512,4,64]{0,2,1:T(8,128)(2,1)S(1)}, u32[]{:S(2)}, u32[]{:S(2)}) %all-to-all-start.4) | async-done | bytes 262176 | tf_op jit(solution)/shard_map/all_to_all | solution.py:93
  118.2 97.1 %while.23 = (s32[]{:T(128)}, f32[32,128,128]{2,1,0:T(8,128)}, bf16[4,4,128,1,64]{2,4,1,3,0:T(8,128)(2,1)}, s32[4,4,12]{2,1,0:T(4,128)S(1)}, bf16[4,4,128,1,64]{2...) while((s32[]{:T(128)}, f32[32,128,128]{2,1,0:T(8,128)}, ...), condition=%wide.region_11.12_spmd, body=%wide.region_7.11_spmd.sunk | while | flops 520650880 | bytes 70544624 | solution.py:128
  129.8 2.3 copy.150
  132.2 10.3 %scatter_fusion = f32[32,128,128]{2,1,0:T(8,128)} fusion(f32[32,128,128]{2,1,0:T(8,128)} %get-tuple-element.320, s32[48]{0:T(128)S(1)} %fusion.76, f32[48,128,128]{2,1,0:T(8,128)} %copy.150), kind=kCustom, calls=%fused_computation.3.clone.1 | custom fusion | flops 786432 | bytes 9437376 | tf_op jit(solution)/shard_map/while/body/eval_jaxpr/scatter-add | solution.py:124
  156.4 10.3 %scatter_fusion = f32[32,128,128]{2,1,0:T(8,128)} fusion(f32[32,128,128]{2,1,0:T(8,128)} %get-tuple-element.320, s32[48]{0:T(128)S(1)} %fusion.76, f32[48,128,128]{2,1,0:T(8,128)} %copy.150), kind=kCustom, calls=%fused_computation.3.clone.1 | custom fusion | flops 786432 | bytes 9437376 | tf_op jit(solution)/shard_map/while/body/eval_jaxpr/scatter-add | solution.py:124
  180.7 10.3 %scatter_fusion = f32[32,128,128]{2,1,0:T(8,128)} fusion(f32[32,128,128]{2,1,0:T(8,128)} %get-tuple-element.320, s32[48]{0:T(128)S(1)} %fusion.76, f32[48,128,128]{2,1,0:T(8,128)} %copy.150), kind=kCustom, calls=%fused_computation.3.clone.1 | custom fusion | flops 786432 | bytes 9437376 | tf_op jit(solution)/shard_map/while/body/eval_jaxpr/scatter-add | solution.py:124
  205.0 10.3 %scatter_fusion = f32[32,128,128]{2,1,0:T(8,128)} fusion(f32[32,128,128]{2,1,0:T(8,128)} %get-tuple-element.320, s32[48]{0:T(128)S(1)} %fusion.76, f32[48,128,128]{2,1,0:T(8,128)} %copy.150), kind=kCustom, calls=%fused_computation.3.clone.1 | custom fusion | flops 786432 | bytes 9437376 | tf_op jit(solution)/shard_map/while/body/eval_jaxpr/scatter-add | solution.py:124
  217.5 3.8 %all-to-all-start.5 = ((bf16[8,2,128,128]{3,2,1,0:T(8,128)(2,1)}), bf16[8,2,128,128]{3,2,1,0:T(8,128)(2,1)S(1)}, u32[]{:S(2)}, u32[]{:S(2)}) async-start(bf16[8,2,128,128]{3,2,1,0:T(8,128)(2,1)} %bitcast.54), calls=%async_computation.5 | async-start | bytes 1048576 | tf_op jit(solution)/shard_map/all_to_all | solution.py:134
  222.6 13.0 %all-to-all-done.5 = bf16[8,2,128,128]{3,2,1,0:T(8,128)(2,1)S(1)} async-done(((bf16[8,2,128,128]{3,2,1,0:T(8,128)(2,1)}), bf16[8,2,128,128]{3,2,1,0:T(8,128)(2,1)S(1)}, u32[]{:S(2)}, u32[]{:S(2)}) %all-to-all-start.5) | async-done | bytes 524320 | tf_op jit(solution)/shard_map/all_to_all | solution.py:134
  239.7 3.6 all-to-all-start.6
  244.5 10.5 %all-to-all-done.6 = bf16[4,512,192]{1,2,0:T(8,128)(2,1)S(1)} async-done(((bf16[4,512,192]{1,2,0:T(8,128)(2,1)}), bf16[4,512,192]{1,2,0:T(8,128)(2,1)S(1)}, u32[]{:S(2)}, u32[]{:S(2)}) %all-to-all-start.6) | async-done | bytes 786464 | tf_op jit(solution)/shard_map/all_to_all | solution.py:142
  257.2 9.0 %reduce-scatter.5.cloned.1.call-done = f32[64,256]{1,0:T(8,128)} async-done(((f32[256,256]{1,0:T(8,128)}), f32[64,256]{1,0:T(8,128)}) %reduce-scatter.5.cloned.1.call-update) | async-done | bytes 65552 | tf_op jit(solution)/shard_map/reduce_scatter | solution.py:149
  266.2 26.0 %reduce-scatter.3.cloned.1.call-done = f32[256,192]{0,1:T(8,128)} async-done(((f32[256,768]{0,1:T(8,128)}), f32[256,192]{0,1:T(8,128)}) %reduce-scatter.3.cloned.1.call-update) | async-done | bytes 196624 | tf_op jit(solution)/shard_map/reduce_scatter | solution.py:148
  293.5 72.9 %all-reduce.3.cloned.1.call-done = (f32[256,192]{0,1:T(8,128)}, f32[64,256]{1,0:T(8,128)}) async-done(((f32[256,192]{0,1:T(8,128)}, f32[64,256]{1,0:T(8,128)}), (f32[256,192]{0,1:T(8,128)}, f32[64,256]{1,0:T(8,128)})) %all-reduce.3.cloned.1.call-update) | async-done | bytes 262160 | tf_op jit(solution)/shard_map/psum | solution.py:151
  (272 shorter events, 119.1 us)
Async XLA Ops:
  8.6 13.7 %all-to-all-start.1 = ((s32[1,8,2]{2,0,1:T(1,128)}), s32[1,8,2]{2,0,1:T(1,128)S(1)}, u32[]{:S(2)}, u32[]{:S(2)}) async-start(s32[1,8,2]{2,0,1:T(1,128)} %copy.101), calls=%async_computation.1 | async-start | bytes 8192 | tf_op jit(solution)/shard_map/all_to_all | solution.py:45
  22.2 15.1 %all-to-all-start = ((bf16[512,4,192]{0,2,1:T(8,128)(2,1)}), bf16[512,4,192]{0,2,1:T(8,128)(2,1)S(1)}, u32[]{:S(2)}, u32[]{:S(2)}) async-start(bf16[512,4,192]{0,2,1:T(8,128)(2,1)} %bitcast.42), calls=%async_computation | async-start | bytes 1572864 | tf_op jit(solution)/shard_map/all_to_all | solution.py:41
  27.0 10.4 %copy-start.20 = (s32[16]{0:T(128)}, s32[16]{0:T(128)S(1)}, u32[]{:S(2)}) copy-start(s32[16]{0:T(128)S(1)} %fusion.41) | copy-start | bytes 196
  39.9 18.9 %copy-start.17 = (s32[16,12]{1,0:T(8,128)S(1)}, s32[16,12]{1,0:T(8,128)}, u32[]{:S(2)}) copy-start(s32[16,12]{1,0:T(8,128)} %param.15) | copy-start | bytes 2308
  39.9 18.1 %all-to-all-start.2 = ((bf16[8,2,128,128]{2,3,1,0:T(8,128)(2,1)}), bf16[8,2,128,128]{2,3,1,0:T(8,128)(2,1)S(1)}, u32[]{:S(2)}, u32[]{:S(2)}) async-start(bf16[8,2,128,128]{2,3,1,0:T(8,128)(2,1)} %bitcast.46), calls=%async_computation.2 | async-start | bytes 1048576 | tf_op jit(solution)/shard_map/all_to_all | solution.py:47
  58.8 37.3 %copy-start.8 = (bf16[512,256]{1,0:T(8,128)(2,1)S(1)}, bf16[512,256]{1,0:T(8,128)(2,1)}, u32[]{:S(2)}) copy-start(bf16[512,256]{1,0:T(8,128)(2,1)} %param.11) | copy-start | bytes 786436
  90.9 14.3 %copy-start.15 = (bf16[256,256]{1,0:T(8,128)(2,1)S(1)}, bf16[256,256]{1,0:T(8,128)(2,1)}, u32[]{:S(2)}) copy-start(bf16[256,256]{1,0:T(8,128)(2,1)} %param.13) | copy-start | bytes 393220
  92.7 9.4 %all-to-all-start.3 = ((bf16[4,512,64]{1,2,0:T(8,128)(2,1)}), bf16[4,512,64]{1,2,0:T(8,128)(2,1)S(1)}, u32[]{:S(2)}, u32[]{:S(2)}) async-start(bf16[4,512,64]{1,2,0:T(8,128)(2,1)} %all_to_all.70), calls=%async_computation.3 | async-start | bytes 524288 | tf_op jit(solution)/shard_map/all_to_all | solution.py:77
  102.1 16.1 %copy-start.10 = (bf16[4,512,64]{1,2,0:T(8,128)(2,1)}, bf16[4,512,64]{1,2,0:T(8,128)(2,1)S(1)}, u32[]{:S(2)}) copy-start(bf16[4,512,64]{1,2,0:T(8,128)(2,1)S(1)} %all-to-all-done.3) | copy-start | bytes 786436
  106.1 9.4 %all-to-all-start.4 = ((bf16[512,4,64]{0,2,1:T(8,128)(2,1)}), bf16[512,4,64]{0,2,1:T(8,128)(2,1)S(1)}, u32[]{:S(2)}, u32[]{:S(2)}) async-start(bf16[512,4,64]{0,2,1:T(8,128)(2,1)} %bitcast.51), calls=%async_computation.4 | async-start | bytes 524288 | tf_op jit(solution)/shard_map/all_to_all | solution.py:93
  132.2 10.3 %copy-start.13 = (bf16[4,4,128,1,64]{2,1,4,0,3:T(4,128)(2,1)S(1)}, bf16[4,4,128,1,64]{2,1,4,0,3:T(4,128)(2,1)}, u32[]{:S(2)}) copy-start(bf16[4,4,128,1,64]{2,1,4,0,3:T(4,128)(2,1)} %copy-done.12) | copy-start | bytes 786436 | tf_op jit(solution)/shard_map/while
  132.2 10.3 %copy-start.19 = (f32[4,4,128,1]{2,1,3,0:T(4,128)S(1)}, f32[4,4,128,1]{2,1,3,0:T(4,128)}, u32[]{:S(2)}) copy-start(f32[4,4,128,1]{2,1,3,0:T(4,128)} %copy-done.18) | copy-start | bytes 24580 | tf_op jit(solution)/shard_map/while
  205.0 10.3 %copy-start.2 = (bf16[32,128,128]{2,1,0:T(8,128)(2,1)S(1)}, bf16[32,128,128]{2,1,0:T(8,128)(2,1)}, u32[]{:S(2)}) copy-start(bf16[32,128,128]{2,1,0:T(8,128)(2,1)} %copy-done.1) | copy-start | bytes 3145732 | tf_op jit(solution)/shard_map/while
  205.0 10.3 %copy-start.7 = (bf16[4,4,128,1,64]{2,4,1,3,0:T(8,128)(2,1)S(1)}, bf16[4,4,128,1,64]{2,4,1,3,0:T(8,128)(2,1)}, u32[]{:S(2)}) copy-start(bf16[4,4,128,1,64]{2,4,1,3,0:T(8,128)(2,1)} %copy-done.6) | copy-start | bytes 786436 | tf_op jit(solution)/shard_map/while
  205.0 10.3 %copy-start.13 = (bf16[4,4,128,1,64]{2,1,4,0,3:T(4,128)(2,1)S(1)}, bf16[4,4,128,1,64]{2,1,4,0,3:T(4,128)(2,1)}, u32[]{:S(2)}) copy-start(bf16[4,4,128,1,64]{2,1,4,0,3:T(4,128)(2,1)} %copy-done.12) | copy-start | bytes 786436 | tf_op jit(solution)/shard_map/while
  205.0 10.4 %copy-start.19 = (f32[4,4,128,1]{2,1,3,0:T(4,128)S(1)}, f32[4,4,128,1]{2,1,3,0:T(4,128)}, u32[]{:S(2)}) copy-start(f32[4,4,128,1]{2,1,3,0:T(4,128)} %copy-done.18) | copy-start | bytes 24580 | tf_op jit(solution)/shard_map/while
  215.4 20.4 %copy-start.21 = (s32[16]{0:T(128)S(1)}, s32[16]{0:T(128)}, u32[]{:S(2)}) copy-start(s32[16]{0:T(128)} %copy-done.20) | copy-start | bytes 196
  217.5 18.1 %all-to-all-start.5 = ((bf16[8,2,128,128]{3,2,1,0:T(8,128)(2,1)}), bf16[8,2,128,128]{3,2,1,0:T(8,128)(2,1)S(1)}, u32[]{:S(2)}, u32[]{:S(2)}) async-start(bf16[8,2,128,128]{3,2,1,0:T(8,128)(2,1)} %bitcast.54), calls=%async_computation.5 | async-start | bytes 1048576 | tf_op jit(solution)/shard_map/all_to_all | solution.py:134
  238.4 16.6 %copy-start.9 = (bf16[512,256]{1,0:T(8,128)(2,1)S(1)}, bf16[512,256]{1,0:T(8,128)(2,1)}, u32[]{:S(2)}) copy-start(bf16[512,256]{1,0:T(8,128)(2,1)} %param.11) | copy-start | bytes 786436
  239.7 16.6 %copy-start.14 = (bf16[512,256]{0,1:T(8,128)(2,1)S(1)}, bf16[512,256]{0,1:T(8,128)(2,1)}, u32[]{:S(2)}) copy-start(bf16[512,256]{0,1:T(8,128)(2,1)} %get-tuple-element.185) | copy-start | bytes 786436
  239.7 15.3 %all-to-all-start.6 = ((bf16[4,512,192]{1,2,0:T(8,128)(2,1)}), bf16[4,512,192]{1,2,0:T(8,128)(2,1)S(1)}, u32[]{:S(2)}, u32[]{:S(2)}) async-start(bf16[4,512,192]{1,2,0:T(8,128)(2,1)} %copy.111), calls=%async_computation.6 | async-start | bytes 1572864 | tf_op jit(solution)/shard_map/all_to_all | solution.py:142
  243.4 22.9 %reduce-scatter.5.cloned.1.call-start = ((), (), s32[]{:S(2)}) async-start(), calls=%async_computation.10 | async-start | bytes 327680 | tf_op jit(solution)/shard_map/reduce_scatter | solution.py:149
  244.4 47.8 %reduce-scatter.3.cloned.1.call-start = ((), (), s32[]{:S(2)}) async-start(), calls=%async_computation.9 | async-start | bytes 983040 | tf_op jit(solution)/shard_map/reduce_scatter | solution.py:148
  256.3 110.1 %all-reduce.3.cloned.1.call-start = ((), (), s32[]{:S(2)}) async-start(), calls=%async_computation.11 | async-start | bytes 524288 | tf_op jit(solution)/shard_map/psum | solution.py:151
  (36 other events, 210.4 us)
Sparse Core Ops, SparseCore 0:
  246.7 19.5 reduce-scatter.4
  268.9 23.2 reduce-scatter.2
  295.6 70.6 all-reduce.2
where the time goes:
time: 378 us; the launch traced here: 376 us
  waiting for transfers between devices  170 us (45%)
  local copies, waits for them, and re-layouts  64.2 us (17%)
  other arithmetic  58 us (15%)
  matrix products  40.4 us (11%)
  starting transfers between devices  28.9 us (8%)
  between operations  14.1 us (4%)
    psum x1, waiting for transfers between devices, on_device(): lax.psum((in_weight_grad, out_weight_grad), 'node')  72.9 us
    scatter-add x4, other arithmetic, backward_step(): accumulated = accumulated.at[slots.reshape(-1)].add(pair_grads)  41.3 us
    reduce_scatter x1, waiting for transfers between devices, on_device(): lax.psum_scatter(in_weight_grad, 'head', scatter_dimension=1, tiled=True)  26 us
    gather x16, local copies, waits for them, and re-layouts, fetch_keys(): table[slots.reshape(-1)].reshape(group_size, PER, BLOCK, local_heads, 2, HD)  25.4 us
    all_to_all x1, waiting for transfers between devices, on_device(): lax.all_to_all(outgoing, 'node', split_axis=0, concat_axis=0, tiled=True)  13.6 us
    all_to_all x1, waiting for transfers between devices, on_device(): lax.all_to_all(leaving, 'node', split_axis=0, concat_axis=0, tiled=True)  13 us
    dot_general x8, matrix products, attention_weights(): jnp.einsum('gqhd,gpkhd->ghqpk', query_block, key_block, preferred_element...  12.6 us
    all_to_all x1, waiting for transfers between devices, on_device(): lax.all_to_all(projected_grad, 'head', split_axis=0, concat_axis=1, tiled...  10.5 us
  transfers between devices with their start and end apart: 10, of which 10 were waited for; matrix products, arithmetic and copies ran while one was open for 3% of the time, Pallas kernels for 0%

commit v1 on v0

v1 whole, which is shorter than its diff:
```python
import functools
import math

import jax
import jax.numpy as jnp
from jax import lax
from jax.experimental import pallas as pl
from jax.experimental.pallas import tpu as pltpu
from jax.sharding import PartitionSpec as P

HEADS = 4
HD = 64
BLOCK = 128
BLK = 16
PER = 12
CAP = 2
D = 256
PAIRS = BLK // 2
SCALE = HD ** (-0.5)
SCALE_LOG2E = SCALE * math.log2(math.e)
BF16 = jnp.bfloat16
F32 = jnp.float32
MIB = 1 << 20
LAST = (((1,), (1,)), ((), ()))


def dot(a, b):
    return jnp.dot(a, b, preferred_element_type=F32)


def dot_last(a, b):
    return lax.dot_general(a, b, LAST, preferred_element_type=F32)


def span(start, size):
    return pl.ds(pl.multiple_of(start, size), size)


def smem():
    return pl.BlockSpec(memory_space=pltpu.SMEM)


def vmem():
    return pl.BlockSpec(memory_space=pltpu.VMEM)


def call(kernel, name, outs, in_specs, limit, flops=0, scratch=()):
    return pl.pallas_call(
        kernel,
        name=name,
        out_shape=tuple(jax.ShapeDtypeStruct(shape, kind) for shape, kind in outs),
        in_specs=in_specs,
        out_specs=tuple(vmem() for _ in outs),
        scratch_shapes=scratch,
        compiler_params=pltpu.CompilerParams(vmem_limit_bytes=limit),
        cost_estimate=pl.CostEstimate(flops=flops, bytes_accessed=4 * MIB, transcendentals=0),
    )


def project_kernel(head_ref, req_ref, x0, x1, x2, x3, w_ref, qz_ref, kv_ref, out_ref):
    head = head_ref[0]
    rows = x0.shape[0]
    for part, x_ref in enumerate((x0, x1, x2, x3)):
        at = span((head ^ part) * rows, rows)
        y = dot(x_ref[...], w_ref[...]).astype(BF16)
        qz_ref[at, :] = y[:, :BLOCK]
        kv_ref[at, :] = y[:, BLOCK:]

    @pl.loop(0, out_ref.shape[0])
    def _(i):
        out_ref[i] = kv_ref[span(req_ref[i] * BLOCK, BLOCK), :]


def transpose_kernel(head_ref, x0, x1, x2, x3, kv_ref, xt_ref, kvt_ref):
    head = head_ref[0]
    rows = x0.shape[0]
    for part, x_ref in enumerate((x0, x1, x2, x3)):
        at = span((head ^ part) * rows, rows)
        xt_ref[:, at] = x_ref[...].T
    for i in range(BLK):
        kvt_ref[i] = kv_ref[i * BLOCK : (i + 1) * BLOCK, :].T


def forward_kernel(
    slot_ref, count_ref, qz_ref, kv_ref, kvt_ref, inc_ref,
    att_ref, attt_ref, table_ref, tablet_ref, top_ref, inv_ref,
):
    for i in range(BLK):
        table_ref[i] = kv_ref[i * BLOCK : (i + 1) * BLOCK, :]
        tablet_ref[i] = kvt_ref[i]

    @pl.loop(0, inc_ref.shape[0])
    def _(i):
        block = inc_ref[i]
        table_ref[BLK + i] = block
        tablet_ref[BLK + i] = block.T

    def one(i):
        slots = [slot_ref[i * PER + j] for j in range(PER)]
        count = count_ref[i]
        keys = jnp.concatenate([table_ref[s] for s in slots], axis=0)
        raw = dot_last(keys, qz_ref[span(i * BLOCK, BLOCK), :])
        raw = jnp.concatenate(
            [
                jnp.where(j < count, raw[j * BLOCK : (j + 1) * BLOCK], -1e30)
                for j in range(PER)
            ],
            axis=0,
        )
        top = jnp.max(raw, axis=0, keepdims=True)
        raised = jnp.exp2((raw - top) * SCALE_LOG2E)
        inverse = 1.0 / jnp.sum(raised, axis=0, keepdims=True)
        low = (raised * inverse).astype(BF16)
        values = jnp.concatenate([tablet_ref[s, HD:, :] for s in slots], axis=1)
        result = dot(values, low)
        attt_ref[:, span(i * BLOCK, BLOCK)] = result.astype(BF16)
        top_ref[i] = jnp.broadcast_to(top, (8, BLOCK))
        inv_ref[i] = jnp.broadcast_to(inverse, (8, BLOCK))
        return result

    @pl.loop(0, PAIRS)
    def _(t):
        first = one(2 * t)
        second = one(2 * t + 1)
        both = jnp.concatenate([first, second], axis=0)
        att_ref[span(t * BLOCK, BLOCK), :] = both.T.astype(BF16)


def middle_kernel(
    head_ref, x0, x1, x2, x3, c0, c1, c2, c3, a0, a1, a2, a3, attt_ref, w_ref,
    out_ref, grad_ref, gz_ref, dots_ref, owg_ref, wide_ref, pad_ref,
):
    head = head_ref[0]
    rows = x0.shape[0]
    own_w = w_ref[span(head * HD, HD), :]
    wide_ref[...] = jnp.zeros_like(wide_ref)
    for part in range(4):
        piece = w_ref[span((head ^ part) * HD, HD), :]
        at = (2 * part) * HD
        wide_ref[at : at + HD, :D] = piece
        wide_ref[at + HD : at + 2 * HD, D:] = piece
    pad_ref[:HD, :] = jnp.zeros((HD, D), BF16)
    pad_ref[HD:, :] = own_w
    a_refs = (a0, a1, a2, a3)
    owg = jnp.zeros((HD, D), F32)
    for part, (x_ref, c_ref) in enumerate(zip((x0, x1, x2, x3), (c0, c1, c2, c3))):
        group = head ^ part
        for pair in range(rows // (2 * BLOCK)):
            t = group * (rows // (2 * BLOCK)) + pair
            lhs = jnp.concatenate([a[span(t * BLOCK, BLOCK), :] for a in a_refs], axis=1)
            product = dot(lhs, wide_ref[...])
            for half in range(2):
                local = (2 * pair + half) * BLOCK
                block = 2 * t + half
                at = span(block * BLOCK, BLOCK)
                summed = x_ref[local : local + BLOCK, :].astype(F32) + product[:, half * D : (half + 1) * D]
                inverse = lax.rsqrt(jnp.mean(summed * summed, axis=-1, keepdims=True) + 1e-06)
                normed = summed * inverse
                upstream = c_ref[local : local + BLOCK, :].astype(F32)
                grad = (upstream - normed * jnp.mean(upstream * normed, axis=-1, keepdims=True)) * inverse
                low = grad.astype(BF16)
                if part == 0:
                    out_ref[local : local + BLOCK, :] = normed.astype(BF16)
                    grad_ref[local : local + BLOCK, :] = grad
                gz_ref[at, :] = dot_last(low, pad_ref[...]).astype(BF16)
                turned = dot_last(own_w, low).astype(BF16).astype(F32)
                attended = attt_ref[:, at]
                sums = jnp.sum(turned * attended.astype(F32), axis=0, keepdims=True)
                dots_ref[block] = jnp.broadcast_to(sums, (8, BLOCK))
                owg += dot(attended, low)
    owg_ref[...] = owg


def backward_kernel(
    slot_ref, count_ref, qz_ref, gz_ref, table_ref, tablet_ref, top_ref, inv_ref, dots_ref,
    own_ref, leave_ref, dq_ref, dqt_ref, acc_ref,
):
    acc_ref[...] = jnp.zeros_like(acc_ref)

    def one(i):
        slots = [slot_ref[i * PER + j] for j in range(PER)]
        count = count_ref[i]
        at = span(i * BLOCK, BLOCK)
        keys = jnp.concatenate([table_ref[s] for s in slots], axis=0)
        rows = jnp.concatenate([qz_ref[at, :], gz_ref[at, :]], axis=0)
        both = dot_last(keys, rows)
        top = top_ref[i, :1, :]
        inverse = inv_ref[i, :1, :]
        dots = dots_ref[i, :1, :]
        weights, grads = [], []
        for j in range(PER):
            here = both[j * BLOCK : (j + 1) * BLOCK]
            weight = jnp.exp2((here[:, :BLOCK] - top) * SCALE_LOG2E) * inverse
            weight = jnp.where(j < count, weight, 0.0)
            weights.append(weight.astype(BF16))
            grads.append((weight * (here[:, BLOCK:] - dots) * SCALE).astype(BF16))
        score_grad = jnp.concatenate(grads, axis=0)
        low = jnp.concatenate(weights, axis=0)
        pair_grads = dot(jnp.concatenate([score_grad, low], axis=1), rows)
        for j in range(PER):
            acc_ref[slots[j]] += pair_grads[j * BLOCK : (j + 1) * BLOCK]
        turned = jnp.concatenate([tablet_ref[s, :HD, :] for s in slots], axis=1)
        result = dot(turned, score_grad)
        dqt_ref[:, at] = result.astype(BF16)
        return result

    @pl.loop(0, PAIRS)
    def _(t):
        first = one(2 * t)
        second = one(2 * t + 1)
        both = jnp.concatenate([first, second], axis=0)
        dq_ref[span(t * BLOCK, BLOCK), :] = both.T.astype(BF16)

    own_ref[...] = acc_ref[:BLK]

    @pl.loop(0, leave_ref.shape[0])
    def _(i):
        leave_ref[i] = acc_ref[BLK + i].astype(BF16)


def query_weight_kernel(head_ref, dqt_ref, x0, x1, x2, x3, out_ref):
    head = head_ref[0]
    rows = x0.shape[0]
    total = jnp.zeros((HD, D), F32)
    for part, x_ref in enumerate((x0, x1, x2, x3)):
        total += dot(dqt_ref[:, span((head ^ part) * rows, rows)], x_ref[...])
    out_ref[...] = total


def collect_kernel(req_ref, own_ref, back_ref, xt_ref, kvg_ref, wg_ref, sum_ref):
    sum_ref[...] = own_ref[...]

    @pl.loop(0, back_ref.shape[0])
    def _(i):
        sum_ref[req_ref[i]] += back_ref[i].astype(F32)

    for i in range(BLK):
        kvg_ref[i * BLOCK : (i + 1) * BLOCK, :] = sum_ref[i].astype(BF16)
    wg_ref[...] = dot(xt_ref[...], kvg_ref[...])


def finish_kernel(grad_ref, dq_ref, kv_ref, wq_ref, wkv_ref, out_ref):
    rows = out_ref.shape[0]
    kv = jnp.concatenate([kv_ref[g] for g in range(4)], axis=1)
    base = grad_ref[...] + dot(kv, wkv_ref[...])
    for pair in range(rows // (2 * BLOCK)):
        lhs = jnp.concatenate(
            [dq_ref[g, pair * BLOCK : (pair + 1) * BLOCK, :] for g in range(4)], axis=1
        )
        product = dot(lhs, wq_ref[...])
        for half in range(2):
            at = (2 * pair + half) * BLOCK
            out_ref[at : at + BLOCK, :] = (
                base[at : at + BLOCK] + product[:, half * D : (half + 1) * D]
            ).astype(BF16)


def on_device(features, in_weight, out_weight, cotangent, key_slots, block_count, wanted):
    head_count = lax.axis_size("head")
    node_count = lax.axis_size("node")
    rows = features.shape[0]
    node_rows = rows * head_count
    total_nodes = node_rows * node_count
    remote = node_count * CAP
    table_size = BLK + remote
    limit = (14 + table_size // 4) * MIB
    head = lax.axis_index("head")
    head_word = head.astype(jnp.int32).reshape(1)

    def swap(value, axis, mask):
        size = lax.axis_size(axis)
        return lax.ppermute(value, axis, [(i, i ^ mask) for i in range(size)])

    def gather_heads(value):
        across = swap(value, "head", 2)
        beside = swap(value, "head", 1)
        return (value, beside, across, swap(across, "head", 1))

    def add_nodes(value):
        mask = 1
        while mask < node_count:
            value = value + swap(value, "node", mask)
            mask *= 2
        return value

    xs = gather_heads(features)
    requests = lax.all_to_all(
        wanted.reshape(node_count, CAP), "node", split_axis=0, concat_axis=0, tiled=True
    ).reshape(-1)
    own_in = lax.dynamic_slice(in_weight, (0, head * (3 * HD)), (D, 3 * HD))
    wide_in = jnp.concatenate([own_in[:, :HD], jnp.zeros((D, HD), BF16), own_in[:, HD:]], axis=1)
    in_turned = in_weight.T.reshape(HEADS, 3 * HD, D)
    wkv = in_turned[:, HD:].reshape(HEADS * 2 * HD, D)
    wq = in_turned[:, :HD]
    blank = jnp.zeros_like(wq)
    wq = jnp.stack(
        [jnp.concatenate([wq, blank], axis=2), jnp.concatenate([blank, wq], axis=2)], axis=1
    ).reshape(HEADS * 2 * HD, 2 * D)
    slots = key_slots.reshape(-1)

    qz, kv, outgoing = call(
        project_kernel,
        "project",
        [
            ((node_rows, BLOCK), BF16),
            ((node_rows, BLOCK), BF16),
            ((remote, BLOCK, BLOCK), BF16),
        ],
        [smem(), smem()] + [vmem()] * 5,
        limit,
        flops=2 * node_rows * D * D,
    )(head_word, requests, *xs, wide_in)
    incoming = lax.all_to_all(outgoing, "node", split_axis=0, concat_axis=0, tiled=True)
    cs = gather_heads(cotangent)
    xt, kvt = call(
        transpose_kernel,
        "transpose",
        [((D, node_rows), BF16), ((BLK, BLOCK, BLOCK), BF16)],
        [smem()] + [vmem()] * 5,
        limit,
        flops=2 * node_rows * D * D,
    )(head_word, *xs, kv)
    att, attt, table, tablet, top, inv = call(
        forward_kernel,
        "forward",
        [
            ((PAIRS * BLOCK, BLOCK), BF16),
            ((HD, node_rows), BF16),
            ((table_size, BLOCK, BLOCK), BF16),
            ((table_size, BLOCK, BLOCK), BF16),
            ((BLK, 8, BLOCK), F32),
            ((BLK, 8, BLOCK), F32),
        ],
        [smem(), smem()] + [vmem()] * 4,
        limit,
        flops=4 * node_rows * PER * BLOCK * BLOCK,
    )(slots, block_count, qz, kv, kvt, incoming)
    parts = gather_heads(att)
    output, norm_grad, gz, dots, owg = call(
        middle_kernel,
        "middle",
        [
            ((rows, D), BF16),
            ((rows, D), F32),
            ((node_rows, BLOCK), BF16),
            ((BLK, 8, BLOCK), F32),
            ((HD, D), F32),
        ],
        [smem()] + [vmem()] * 14,
        limit,
        flops=8 * node_rows * D * D,
        scratch=[pltpu.VMEM((2 * D, 2 * D), BF16), pltpu.VMEM((BLOCK, D), BF16)],
    )(head_word, *xs, *cs, *parts, attt, out_weight)
    own, leaving, dq, dqt = call(
        backward_kernel,
        "backward",
        [
            ((BLK, BLOCK, BLOCK), F32),
            ((remote, BLOCK, BLOCK), BF16),
            ((PAIRS * BLOCK, BLOCK), BF16),
            ((HD, node_rows), BF16),
        ],
        [smem(), smem()] + [vmem()] * 7,
        limit,
        flops=10 * node_rows * PER * BLOCK * BLOCK,
        scratch=[pltpu.VMEM((table_size, BLOCK, BLOCK), F32)],
    )(slots, block_count, qz, gz, table, tablet, top, inv, dots)
    returned = lax.all_to_all(leaving, "node", split_axis=0, concat_axis=0, tiled=True)
    dq_rows = lax.all_to_all(
        dq.reshape(head_count, rows // 2, BLOCK), "head", split_axis=0, concat_axis=0, tiled=True
    )
    (query_wg,) = call(
        query_weight_kernel,
        "query_weight",
        [((HD, D), F32)],
        [smem()] + [vmem()] * 5,
        limit,
        flops=2 * node_rows * D * HD,
    )(head_word, dqt, *xs)
    kvg, pair_wg = call(
        collect_kernel,
        "collect",
        [((node_rows, BLOCK), BF16), ((D, BLOCK), F32)],
        [smem()] + [vmem()] * 3,
        limit,
        flops=2 * node_rows * D * BLOCK,
        scratch=[pltpu.VMEM((BLK, BLOCK, BLOCK), F32)],
    )(requests, own, returned, xt)
    kv_rows = lax.all_to_all(
        kvg.reshape(head_count, rows, BLOCK), "head", split_axis=0, concat_axis=0, tiled=True
    )
    (feature_grad,) = call(
        finish_kernel,
        "finish",
        [((rows, D), BF16)],
        [vmem()] * 5,
        limit,
        flops=4 * rows * 3 * D * D,
    )(norm_grad, dq_rows, kv_rows, wq, wkv)
    owg = add_nodes(owg)
    query_wg = add_nodes(query_wg)
    pair_wg = add_nodes(pair_wg)
    grad_factor = total_nodes ** (-0.5)
    return (
        output,
        feature_grad,
        jnp.concatenate([query_wg.T, pair_wg], axis=1) * grad_factor,
        owg * grad_factor,
    )


def solution(mesh):
    placed = (
        P(("node", "head"), None),
        P(),
        P(),
        P(("node", "head"), None),
        P("node", None),
        P("node"),
        P("node", None, None),
    )
    return jax.shard_map(
        on_device,
        mesh=mesh,
        in_specs=placed,
        out_specs=(
            P(("node", "head"), None),
            P(("node", "head"), None),
            P(None, "head"),
            P("head", None),
        ),
        check_vma=False,
    )
```

time: 378 us -> 133 us (0.35)
  waiting for transfers between devices: 170 us -> 39.3 us
  other arithmetic: 58 us -> 3.95 us
  local copies, waits for them, and re-layouts: 64.2 us -> 13.9 us
  matrix products: 40.4 us -> 0 us
  Pallas kernels: 0 us -> 38.4 us
  between operations: 14.1 us -> 0.9 us
  starting transfers between devices: 28.9 us -> 35.8 us
    psum x1 -> x0, waiting for transfers between devices: 72.9 us -> none  [on_device(): lax.psum((in_weight_grad, out_weight_grad), 'node')]
    scatter-add x5 -> x0, other arithmetic: 42.9 us -> none  [the longest x4 41.3 us: backward_step(): accumulated = accumulated.at[slots.reshape(-1)].add(pair_grads)]
    dot_general x34 -> x0, matrix products: 40.4 us -> none  [the longest x8 12.6 us: attention_weights(): jnp.einsum('gqhd,gpkhd->ghqpk', query_block, key_block, preferred_element...]
    pallas_call x0 -> x8, Pallas kernels: none -> 38.4 us  [the longest x1 15 us: on_device(): call(forward_kernel, 'forward', [((PAIRS * BLOCK, BLOCK), BF16), ((HD, no...]
    reduce_scatter x2 -> x0, waiting for transfers between devices: 35 us -> none  [the longest x1 26 us: on_device(): lax.psum_scatter(in_weight_grad, 'head', scatter_dimension=1, tiled=True)]
    all_to_all x5 -> x3, waiting for transfers between devices: 35.3 us -> 4 us  [the longest x1 3.99 us: on_device(): lax.all_to_all(wanted.reshape(node_count, CAP), 'node', split_axis=0, con...]
    gather x17 -> x0, local copies, waits for them, and re-layouts: 26.8 us -> none  [the longest x16 25.4 us: fetch_keys(): table[slots.reshape(-1)].reshape(group_size, PER, BLOCK, local_heads, 2, HD)]
    ppermute x0 -> x18, waiting for transfers between devices: none -> 17.5 us  [swap(): return lax.ppermute(value, axis, [(i, i ^ mask) for i in range(size)])]
  transfers between devices with their start and end apart: 10 -> 23, of which waited for: 10 -> 9; matrix products, arithmetic and copies ran while one was open for 3% -> 9% of each run, Pallas kernels for 0% -> 13%
where the time goes in v1:
time: 133 us; the launch traced here: 132 us
  waiting for transfers between devices  39.3 us (30%)
  Pallas kernels  38.4 us (29%)
  starting transfers between devices  35.8 us (27%)
  local copies, waits for them, and re-layouts  13.9 us (10%)
  other arithmetic  3.95 us (3%)
    ppermute x18, waiting for transfers between devices, swap(): return lax.ppermute(value, axis, [(i, i ^ mask) for i in range(size)])  17.5 us
    pallas_call x1, Pallas kernels, on_device(): call(forward_kernel, 'forward', [((PAIRS * BLOCK, BLOCK), BF16), ((HD, no...  15 us
    ppermute x18, starting transfers between devices, swap(): return lax.ppermute(value, axis, [(i, i ^ mask) for i in range(size)])  14.7 us
    pallas_call x1, Pallas kernels, on_device(): call(backward_kernel, 'backward', [((BLK, BLOCK, BLOCK), F32), ((remote,...  12.4 us
    all_to_all x1, waiting for transfers between devices, on_device(): lax.all_to_all(outgoing, 'node', split_axis=0, concat_axis=0, tiled=True)  11.9 us
    unnamed x32, local copies, waits for them, and re-layouts  8.78 us
    all_to_all x1, waiting for transfers between devices, on_device(): lax.all_to_all(leaving, 'node', split_axis=0, concat_axis=0, tiled=True)  5.9 us
    all_to_all x1, starting transfers between devices, on_device(): lax.all_to_all(wanted.reshape(node_count, CAP), 'node', split_axis=0, con...  5.83 us
  transfers between devices with their start and end apart: 23, of which 9 were waited for; matrix products, arithmetic and copies ran while one was open for 9% of the time, Pallas kernels for 13%

profile of v1, /device:TPU:0, one launch (start us, length us, event | category | flops | bytes accessed | tf_op | source)
XLA Modules:
  0.0 132.3 jit_solution(13270927201282770294)
XLA Ops:
  0.6 3.0 %collective-permute-start.1 = (bf16[512,256]{1,0:T(8,128)(2,1)}, bf16[512,256]{1,0:T(8,128)(2,1)S(1)}, u32[]{:S(2)}, u32[]{:S(2)}) collective-permute-start(bf16[512,256]{1,0:T(8,128)(2,1)} %x0.7), channel_id=1, source_target_pairs={{0,2},{1,3},{2,0},{3,1},{4,6},{5,7},{6,4},{7,5},{8,10},{9,11},{10,... | collective-permute-start | bytes 786440 | tf_op jit(solution)/shard_map/ppermute | solution.py:272
  4.3 5.8 %all-to-all-start = ((s32[8,1,2]{2,1,0:T(1,128)}), s32[8,1,2]{2,1,0:T(1,128)S(1)}, u32[]{:S(2)}, u32[]{:S(2)}) async-start(s32[8,1,2]{2,1,0:T(1,128)} %copy.22), calls=%async_computation | async-start | bytes 8192 | tf_op jit(solution)/shard_map/all_to_all | solution.py:287
  12.6 4.0 %all-to-all-done = s32[8,1,2]{2,1,0:T(1,128)S(1)} async-done(((s32[8,1,2]{2,1,0:T(1,128)}), s32[8,1,2]{2,1,0:T(1,128)S(1)}, u32[]{:S(2)}, u32[]{:S(2)}) %all-to-all-start) | async-done | bytes 96 | tf_op jit(solution)/shard_map/all_to_all | solution.py:287
  17.8 2.0 %project.1 = (bf16[2048,128]{1,0:T(8,128)(2,1)S(1)}, bf16[2048,128]{1,0:T(8,128)(2,1)S(1)}, bf16[16,128,128]{2,1,0:T(8,128)(2,1)}) custom-call(s32[1]{0:T(128)} %bitcast.head_ref, s32[16]{0:T(128)S(1)} %reshape.39.req_ref, bf16[512,256]{1,0:T(8,128)(2,1)S(1)} %copy-done, bf16[512,256]{1,0:T(8,128)(2,1)S(1)} %collective-permute-done.x1, ...), custom_call_target="tpu_custom_call" | custom-call | flops 268435456 | bytes 4194304 | tf_op jit(solution)/shard_map/project/pallas_call | solution.py:301
  20.6 3.5 %all-to-all-start.1 = ((bf16[16,128,128]{2,1,0:T(8,128)(2,1)}), bf16[16,128,128]{2,1,0:T(8,128)(2,1)S(1)}, u32[]{:S(2)}, u32[]{:S(2)}) async-start(bf16[16,128,128]{2,1,0:T(8,128)(2,1)} %get-tuple-element.29), calls=%async_computation.1 | async-start | bytes 1048576 | tf_op jit(solution)/shard_map/all_to_all | solution.py:313
  26.1 11.9 %all-to-all-done.1.inc_ref = bf16[16,128,128]{2,1,0:T(8,128)(2,1)S(1)} async-done(((bf16[16,128,128]{2,1,0:T(8,128)(2,1)}), bf16[16,128,128]{2,1,0:T(8,128)(2,1)S(1)}, u32[]{:S(2)}, u32[]{:S(2)}) %all-to-all-start.1) | async-done | bytes 524320 | tf_op jit(solution)/shard_map/all_to_all | solution.py:313
  40.8 15.0 %forward.1 = (bf16[1024,128]{1,0:T(8,128)(2,1)S(1)}, bf16[64,2048]{1,0:T(8,128)(2,1)S(1)}, bf16[32,128,128]{2,1,0:T(8,128)(2,1)S(1)}, bf16[32,128,128]{2,1,0:T(8...) custom-call(s32[192]{0:T(256)S(1)} %reshape.38.slot_ref, s32[16]{0:T(128)S(1)} %copy-done.10, ...), custom_call_target="tpu_custom_call" | custom-call | flops 1610612736 | bytes 4194304 | tf_op jit(solution)/shard_map/forward/pallas_call | solution.py:323
  56.9 5.5 %collective-permute-done.7.a2 = bf16[1024,128]{1,0:T(8,128)(2,1)S(1)} collective-permute-done((bf16[1024,128]{1,0:T(8,128)(2,1)S(1)}, bf16[1024,128]{1,0:T(8,128)(2,1)S(1)}, u32[]{:S(2)}, u32[]{:S(2)}) %collective-permute-start.7) | collective-permute-done | bytes 262176 | tf_op jit(solution)/shard_map/ppermute | solution.py:272
  62.4 1.5 %collective-permute-done.8.a3 = bf16[1024,128]{1,0:T(8,128)(2,1)S(1)} collective-permute-done((bf16[1024,128]{1,0:T(8,128)(2,1)S(1)}, bf16[1024,128]{1,0:T(8,128)(2,1)S(1)}, u32[]{:S(2)}, u32[]{:S(2)}) %collective-permute-start.8) | collective-permute-done | bytes 262176 | tf_op jit(solution)/shard_map/ppermute | solution.py:272
  63.9 5.3 %middle.1 = (bf16[512,256]{1,0:T(8,128)(2,1)}, f32[512,256]{1,0:T(8,128)S(1)}, bf16[2048,128]{1,0:T(8,128)(2,1)S(1)}, f32[16,8,128]{2,1,0:T(8,128)S(1)}, f32[64,256]{1,0:T(8,128)S(1)}) custom-call(s32[1]{0:T(128)} %bitcast.head_ref, bf16[512,256]{1,0:T(8,128)(2,1)S(1)} %copy-done, bf16[512,256]{1,0:T(8,128)(2,1)S(1)} %collective-permute-done.x1, ...), custom_call_target="tpu_custom_call" | custom-call | flops 1073741824 | bytes 4194304 | tf_op jit(solution)/shard_map/middle/pallas_call | solution.py:339
  69.2 12.4 %backward.1 = (f32[16,128,128]{2,1,0:T(8,128)S(1)}, bf16[16,128,128]{2,1,0:T(8,128)(2,1)}, bf16[1024,128]{1,0:T(8,128)(2,1)S(1)}, bf16[64,2048]{1,0:T(8,128)(2,1)S(1)}) custom-call(s32[192]{0:T(256)S(1)} %reshape.38.slot_ref, s32[16]{0:T(128)S(1)} %copy-done.10, bf16[2048,128]{1,0:T(8,128)(2,1)S(1)} %copy-done.6, ...), custom_call_target="tpu_custom_call" | custom-call | flops 4026531840 | bytes 4194304 | tf_op jit(solution)/shard_map/backward/pallas_call | solution.py:354
  83.3 4.9 %all-to-all-start.3 = ((bf16[16,128,128]{2,1,0:T(8,128)(2,1)}), bf16[16,128,128]{2,1,0:T(8,128)(2,1)S(1)}, u32[]{:S(2)}, u32[]{:S(2)}) async-start(bf16[16,128,128]{2,1,0:T(8,128)(2,1)} %get-tuple-element.42), calls=%async_computation.3 | async-start | bytes 1048576 | tf_op jit(solution)/shard_map/all_to_all | solution.py:368
  88.5 2.1 %collective-permute-start.9 = (f32[64,256]{1,0:T(8,128)S(1)}, f32[64,256]{1,0:T(8,128)S(1)}, u32[]{:S(2)}, u32[]{:S(2)}) collective-permute-start(f32[64,256]{1,0:T(8,128)S(1)} %query_weight.1), channel_id=1, source_target_pairs={{0,4},{4,0},{8,12},{12,8},{16,20},{20,16},{24,28},{28,24},{1,5},{5... | collective-permute-start | bytes 196616 | tf_op jit(solution)/shard_map/ppermute | solution.py:272
  90.6 1.9 %copy.23 = bf16[256,768]{0,1:T(8,128)(2,1)} copy(bf16[256,768]{1,0:T(8,128)(2,1)} %param.8) | data formatting | bytes 786432 | tf_op args[1]
  92.5 1.6 %slice.16 = bf16[4,64,256]{2,1,0:T(8,128)(2,1)} slice(bf16[4,192,256]{2,1,0:T(8,128)(2,1)} %bitcast.18), slice={[0:4], [0:64], [0:256]} | slice | bytes 262144 | tf_op jit(solution)/shard_map/slice | solution.py:294
  94.1 1.9 %collective-permute-done.9 = f32[64,256]{1,0:T(8,128)S(1)} collective-permute-done((f32[64,256]{1,0:T(8,128)S(1)}, f32[64,256]{1,0:T(8,128)S(1)}, u32[]{:S(2)}, u32[]{:S(2)}) %collective-permute-start.9) | collective-permute-done | bytes 65568 | tf_op jit(solution)/shard_map/ppermute | solution.py:272
  97.0 5.9 %all-to-all-done.3.back_ref = bf16[16,128,128]{2,1,0:T(8,128)(2,1)S(1)} async-done(((bf16[16,128,128]{2,1,0:T(8,128)(2,1)}), bf16[16,128,128]{2,1,0:T(8,128)(2,1)S(1)}, u32[]{:S(2)}, u32[]{:S(2)}) %all-to-all-start.3) | async-done | bytes 524320 | tf_op jit(solution)/shard_map/all_to_all | solution.py:368
  102.9 3.4 %all-to-all-start.2 = ((bf16[4,256,128]{2,1,0:T(8,128)(2,1)}), bf16[4,256,128]{2,1,0:T(8,128)(2,1)S(1)}, u32[]{:S(2)}, u32[]{:S(2)}) async-start(bf16[4,256,128]{2,1,0:T(8,128)(2,1)} %bitcast.17), calls=%async_computation.2 | async-start | bytes 524288 | tf_op jit(solution)/shard_map/all_to_all | solution.py:369
  106.4 1.9 %collect.1 = (bf16[2048,128]{1,0:T(8,128)(2,1)}, f32[256,128]{1,0:T(8,128)S(1)}) custom-call(s32[16]{0:T(128)S(1)} %reshape.39.req_ref, f32[16,128,128]{2,1,0:T(8,128)S(1)} %copy-done.2, bf16[16,128,128]{2,1,0:T(8,128)(2,1)S(1)} %all-to-all-done.3.back_ref, bf16[256,2048]{1,0:T(8,128)(2,1)S(1)} %get-tuple-element.43.xt_ref), custom_call_target="tpu_custom_call" | custom-call | flops 134217728 | bytes 4194304 | tf_op jit(solution)/shard_map/collect/pallas_call | solution.py:380
  108.3 1.5 %collective-permute-start.12 = (f32[256,128]{1,0:T(8,128)S(1)}, f32[256,128]{1,0:T(8,128)S(1)}, u32[]{:S(2)}, u32[]{:S(2)}) collective-permute-start(f32[256,128]{1,0:T(8,128)S(1)} %get-tuple-element.46), channel_id=1, source_target_pairs={{0,4},{4,0},{8,12},{12,8},{16,20},{20,16},{24,28},{28,24},{1,5},{5... | collective-permute-start | bytes 393224 | tf_op jit(solution)/shard_map/ppermute | solution.py:272
  111.9 1.9 %collective-permute-start.11 = (f32[64,256]{1,0:T(8,128)S(1)}, f32[64,256]{1,0:T(8,128)S(1)}, u32[]{:S(2)}, u32[]{:S(2)}) collective-permute-start(f32[64,256]{1,0:T(8,128)S(1)} %add.36), channel_id=1, source_target_pairs={{0,16},{4,20},{8,24},{12,28},{16,0},{20,4},{24,8},{28,12},{1,17},{... | collective-permute-start | bytes 196616 | tf_op jit(solution)/shard_map/ppermute | solution.py:272
  115.4 1.9 %collective-permute-start.13 = (f32[256,128]{1,0:T(8,128)S(1)}, f32[256,128]{1,0:T(8,128)S(1)}, u32[]{:S(2)}, u32[]{:S(2)}) collective-permute-start(f32[256,128]{1,0:T(8,128)S(1)} %add.38), channel_id=1, source_target_pairs={{0,8},{4,12},{8,0},{12,4},{16,24},{20,28},{24,16},{28,20},{1,9},{5... | collective-permute-start | bytes 393224 | tf_op jit(solution)/shard_map/ppermute | solution.py:272
  117.3 3.5 %all-to-all-start.4 = ((bf16[4,512,128]{2,1,0:T(8,128)(2,1)}), bf16[4,512,128]{2,1,0:T(8,128)(2,1)S(1)}, u32[]{:S(2)}, u32[]{:S(2)}) async-start(bf16[4,512,128]{2,1,0:T(8,128)(2,1)} %bitcast.3), calls=%async_computation.4 | async-start | bytes 1048576 | tf_op jit(solution)/shard_map/all_to_all | solution.py:389
  123.9 6.3 %collective-permute-done.14 = f32[256,128]{1,0:T(8,128)S(1)} collective-permute-done((f32[256,128]{1,0:T(8,128)S(1)}, f32[256,128]{1,0:T(8,128)S(1)}, u32[]{:S(2)}, u32[]{:S(2)}) %collective-permute-start.14) | collective-permute-done | bytes 131104 | tf_op jit(solution)/shard_map/ppermute | solution.py:272
  (88 shorter events, 23.0 us)
Async XLA Ops:
  0.6 10.5 %collective-permute-start.1 = (bf16[512,256]{1,0:T(8,128)(2,1)}, bf16[512,256]{1,0:T(8,128)(2,1)S(1)}, u32[]{:S(2)}, u32[]{:S(2)}) collective-permute-start(bf16[512,256]{1,0:T(8,128)(2,1)} %x0.7), channel_id=1, source_target_pairs={{0,2},{1,3},{2,0},{3,1},{4,6},{5,7},{6,4},{7,5},{8,10},{9,11},{10,... | collective-permute-start | bytes 786440 | tf_op jit(solution)/shard_map/ppermute | solution.py:272
  3.6 14.2 %collective-permute-start = (bf16[512,256]{1,0:T(8,128)(2,1)}, bf16[512,256]{1,0:T(8,128)(2,1)S(1)}, u32[]{:S(2)}, u32[]{:S(2)}) collective-permute-start(bf16[512,256]{1,0:T(8,128)(2,1)} %x0.7), channel_id=1, source_target_pairs={{0,1},{1,0},{2,3},{3,2},{4,5},{5,4},{6,7},{7,6},{8,9},{9,8},{10,11... | collective-permute-start | bytes 786440 | tf_op jit(solution)/shard_map/ppermute | solution.py:272
  4.3 12.2 %all-to-all-start = ((s32[8,1,2]{2,1,0:T(1,128)}), s32[8,1,2]{2,1,0:T(1,128)S(1)}, u32[]{:S(2)}, u32[]{:S(2)}) async-start(s32[8,1,2]{2,1,0:T(1,128)} %copy.22), calls=%async_computation | async-start | bytes 8192 | tf_op jit(solution)/shard_map/all_to_all | solution.py:287
  11.1 6.7 %collective-permute-start.2 = (bf16[512,256]{1,0:T(8,128)(2,1)S(1)}, bf16[512,256]{1,0:T(8,128)(2,1)S(1)}, u32[]{:S(2)}, u32[]{:S(2)}) collective-permute-start(bf16[512,256]{1,0:T(8,128)(2,1)S(1)} %collective-permute-done.1.x2), channel_id=1, source_target_pairs={{0,1},{1,0},{2,3},{3,2},{4,5},{5,4},{6,7},{7,6},{8,9},{9,8},{10,11... | collective-permute-start | bytes 786440 | tf_op jit(solution)/shard_map/ppermute | solution.py:272
  20.6 17.5 %all-to-all-start.1 = ((bf16[16,128,128]{2,1,0:T(8,128)(2,1)}), bf16[16,128,128]{2,1,0:T(8,128)(2,1)S(1)}, u32[]{:S(2)}, u32[]{:S(2)}) async-start(bf16[16,128,128]{2,1,0:T(8,128)(2,1)} %get-tuple-element.29), calls=%async_computation.1 | async-start | bytes 1048576 | tf_op jit(solution)/shard_map/all_to_all | solution.py:313
  24.1 32.3 %collective-permute-start.4 = (bf16[512,256]{1,0:T(8,128)(2,1)}, bf16[512,256]{1,0:T(8,128)(2,1)S(1)}, u32[]{:S(2)}, u32[]{:S(2)}) collective-permute-start(bf16[512,256]{1,0:T(8,128)(2,1)} %c0.1), channel_id=1, source_target_pairs={{0,2},{1,3},{2,0},{3,1},{4,6},{5,7},{6,4},{7,5},{8,10},{9,11},{10,... | collective-permute-start | bytes 786440 | tf_op jit(solution)/shard_map/ppermute | solution.py:272
  40.8 23.1 %copy-start.9 = (bf16[256,256]{1,0:T(8,128)(2,1)S(1)}, bf16[256,256]{1,0:T(8,128)(2,1)}, u32[]{:S(2)}) copy-start(bf16[256,256]{1,0:T(8,128)(2,1)} %w_ref.1) | copy-start | bytes 393220
  55.8 6.6 %collective-permute-start.7 = (bf16[1024,128]{1,0:T(8,128)(2,1)S(1)}, bf16[1024,128]{1,0:T(8,128)(2,1)S(1)}, u32[]{:S(2)}, u32[]{:S(2)}) collective-permute-start(bf16[1024,128]{1,0:T(8,128)(2,1)S(1)} %get-tuple-element.30.a0), channel_id=1, source_target_pairs={{0,2},{1,3},{2,0},{3,1},{4,6},{5,7},{6,4},{7,5},{8,10},{9,11},{10,... | collective-permute-start | bytes 786440 | tf_op jit(solution)/shard_map/ppermute | solution.py:272
  56.4 6.0 %collective-permute-start.3 = (bf16[512,256]{1,0:T(8,128)(2,1)}, bf16[512,256]{1,0:T(8,128)(2,1)S(1)}, u32[]{:S(2)}, u32[]{:S(2)}) collective-permute-start(bf16[512,256]{1,0:T(8,128)(2,1)} %c0.1), channel_id=1, source_target_pairs={{0,1},{1,0},{2,3},{3,2},{4,5},{5,4},{6,7},{7,6},{8,9},{9,8},{10,11... | collective-permute-start | bytes 786440 | tf_op jit(solution)/shard_map/ppermute | solution.py:272
  56.4 6.0 %collective-permute-start.5 = (bf16[512,256]{1,0:T(8,128)(2,1)S(1)}, bf16[512,256]{1,0:T(8,128)(2,1)S(1)}, u32[]{:S(2)}, u32[]{:S(2)}) collective-permute-start(bf16[512,256]{1,0:T(8,128)(2,1)S(1)} %collective-permute-done.4.c2), channel_id=1, source_target_pairs={{0,1},{1,0},{2,3},{3,2},{4,5},{5,4},{6,7},{7,6},{8,9},{9,8},{10,11... | collective-permute-start | bytes 786440 | tf_op jit(solution)/shard_map/ppermute | solution.py:272
  56.9 5.5 %collective-permute-start.6 = (bf16[1024,128]{1,0:T(8,128)(2,1)S(1)}, bf16[1024,128]{1,0:T(8,128)(2,1)S(1)}, u32[]{:S(2)}, u32[]{:S(2)}) collective-permute-start(bf16[1024,128]{1,0:T(8,128)(2,1)S(1)} %get-tuple-element.30.a0), channel_id=1, source_target_pairs={{0,1},{1,0},{2,3},{3,2},{4,5},{5,4},{6,7},{7,6},{8,9},{9,8},{10,11... | collective-permute-start | bytes 786440 | tf_op jit(solution)/shard_map/ppermute | solution.py:272
  62.4 1.5 %collective-permute-start.8 = (bf16[1024,128]{1,0:T(8,128)(2,1)S(1)}, bf16[1024,128]{1,0:T(8,128)(2,1)S(1)}, u32[]{:S(2)}, u32[]{:S(2)}) collective-permute-start(bf16[1024,128]{1,0:T(8,128)(2,1)S(1)} %collective-permute-done.7.a2), channel_id=1, source_target_pairs={{0,1},{1,0},{2,3},{3,2},{4,5},{5,4},{6,7},{7,6},{8,9},{9,8},{10,11... | collective-permute-start | bytes 786440 | tf_op jit(solution)/shard_map/ppermute | solution.py:272
  83.3 19.7 %all-to-all-start.3 = ((bf16[16,128,128]{2,1,0:T(8,128)(2,1)}), bf16[16,128,128]{2,1,0:T(8,128)(2,1)S(1)}, u32[]{:S(2)}, u32[]{:S(2)}) async-start(bf16[16,128,128]{2,1,0:T(8,128)(2,1)} %get-tuple-element.42), calls=%async_computation.3 | async-start | bytes 1048576 | tf_op jit(solution)/shard_map/all_to_all | solution.py:368
  88.5 7.6 %collective-permute-start.9 = (f32[64,256]{1,0:T(8,128)S(1)}, f32[64,256]{1,0:T(8,128)S(1)}, u32[]{:S(2)}, u32[]{:S(2)}) collective-permute-start(f32[64,256]{1,0:T(8,128)S(1)} %query_weight.1), channel_id=1, source_target_pairs={{0,4},{4,0},{8,12},{12,8},{16,20},{20,16},{24,28},{28,24},{1,5},{5... | collective-permute-start | bytes 196616 | tf_op jit(solution)/shard_map/ppermute | solution.py:272
  94.0 15.8 %collective-permute-start.15 = (f32[64,256]{1,0:T(8,128)S(1)}, f32[64,256]{1,0:T(8,128)}, u32[]{:S(2)}, u32[]{:S(2)}) collective-permute-start(f32[64,256]{1,0:T(8,128)S(1)} %get-tuple-element.47), channel_id=1, source_target_pairs={{0,4},{4,0},{8,12},{12,8},{16,20},{20,16},{24,28},{28,24},{1,5},{5... | collective-permute-start | bytes 196616 | tf_op jit(solution)/shard_map/ppermute | solution.py:272
  96.7 14.3 %collective-permute-start.10 = (f32[64,256]{1,0:T(8,128)}, f32[64,256]{1,0:T(8,128)}, u32[]{:S(2)}, u32[]{:S(2)}) collective-permute-start(f32[64,256]{1,0:T(8,128)} %add.35), channel_id=1, source_target_pairs={{0,8},{4,12},{8,0},{12,4},{16,24},{20,28},{24,16},{28,20},{1,9},{5... | collective-permute-start | bytes 196616 | tf_op jit(solution)/shard_map/ppermute | solution.py:272
  102.9 14.3 %all-to-all-start.2 = ((bf16[4,256,128]{2,1,0:T(8,128)(2,1)}), bf16[4,256,128]{2,1,0:T(8,128)(2,1)S(1)}, u32[]{:S(2)}, u32[]{:S(2)}) async-start(bf16[4,256,128]{2,1,0:T(8,128)(2,1)} %bitcast.17), calls=%async_computation.2 | async-start | bytes 524288 | tf_op jit(solution)/shard_map/all_to_all | solution.py:369
  108.3 7.1 %collective-permute-start.12 = (f32[256,128]{1,0:T(8,128)S(1)}, f32[256,128]{1,0:T(8,128)S(1)}, u32[]{:S(2)}, u32[]{:S(2)}) collective-permute-start(f32[256,128]{1,0:T(8,128)S(1)} %get-tuple-element.46), channel_id=1, source_target_pairs={{0,4},{4,0},{8,12},{12,8},{16,20},{20,16},{24,28},{28,24},{1,5},{5... | collective-permute-start | bytes 393224 | tf_op jit(solution)/shard_map/ppermute | solution.py:272
  110.7 4.3 %collective-permute-start.16 = (f32[64,256]{1,0:T(8,128)S(1)}, f32[64,256]{1,0:T(8,128)S(1)}, u32[]{:S(2)}, u32[]{:S(2)}) collective-permute-start(f32[64,256]{1,0:T(8,128)S(1)} %add.41), channel_id=1, source_target_pairs={{0,8},{4,12},{8,0},{12,4},{16,24},{20,28},{24,16},{28,20},{1,9},{5... | collective-permute-start | bytes 196616 | tf_op jit(solution)/shard_map/ppermute | solution.py:272
  111.9 8.9 %collective-permute-start.11 = (f32[64,256]{1,0:T(8,128)S(1)}, f32[64,256]{1,0:T(8,128)S(1)}, u32[]{:S(2)}, u32[]{:S(2)}) collective-permute-start(f32[64,256]{1,0:T(8,128)S(1)} %add.36), channel_id=1, source_target_pairs={{0,16},{4,20},{8,24},{12,28},{16,0},{20,4},{24,8},{28,12},{1,17},{... | collective-permute-start | bytes 196616 | tf_op jit(solution)/shard_map/ppermute | solution.py:272
  115.0 8.2 %collective-permute-start.17 = (f32[64,256]{1,0:T(8,128)S(1)}, f32[64,256]{1,0:T(8,128)S(1)}, u32[]{:S(2)}, u32[]{:S(2)}) collective-permute-start(f32[64,256]{1,0:T(8,128)S(1)} %add.42), channel_id=1, source_target_pairs={{0,16},{4,20},{8,24},{12,28},{16,0},{20,4},{24,8},{28,12},{1,17},{... | collective-permute-start | bytes 196616 | tf_op jit(solution)/shard_map/ppermute | solution.py:272
  115.4 6.6 %collective-permute-start.13 = (f32[256,128]{1,0:T(8,128)S(1)}, f32[256,128]{1,0:T(8,128)S(1)}, u32[]{:S(2)}, u32[]{:S(2)}) collective-permute-start(f32[256,128]{1,0:T(8,128)S(1)} %add.38), channel_id=1, source_target_pairs={{0,8},{4,12},{8,0},{12,4},{16,24},{20,28},{24,16},{28,20},{1,9},{5... | collective-permute-start | bytes 393224 | tf_op jit(solution)/shard_map/ppermute | solution.py:272
  117.3 13.9 %all-to-all-start.4 = ((bf16[4,512,128]{2,1,0:T(8,128)(2,1)}), bf16[4,512,128]{2,1,0:T(8,128)(2,1)S(1)}, u32[]{:S(2)}, u32[]{:S(2)}) async-start(bf16[4,512,128]{2,1,0:T(8,128)(2,1)} %bitcast.3), calls=%async_computation.4 | async-start | bytes 1048576 | tf_op jit(solution)/shard_map/all_to_all | solution.py:389
  122.0 8.2 %collective-permute-start.14 = (f32[256,128]{1,0:T(8,128)S(1)}, f32[256,128]{1,0:T(8,128)S(1)}, u32[]{:S(2)}, u32[]{:S(2)}) collective-permute-start(f32[256,128]{1,0:T(8,128)S(1)} %add.39), channel_id=1, source_target_pairs={{0,16},{4,20},{8,24},{12,28},{16,0},{20,4},{24,8},{28,12},{1,17},{... | collective-permute-start | bytes 393224 | tf_op jit(solution)/shard_map/ppermute | solution.py:272
  (14 other events, 49.8 us)
